TPU v7x, 32 devices: a whole 2x2x4 slice. The times are simulated.
32 devices in a mesh: req: 8 (over z, x), tp: 4 (over y, core).
Axes of the slice: x: 2, y: 2, z: 4, core: 2. Of those that a mesh axis runs over, the one named last changes fastest.
Arguments:
- tokens: bfloat16 [4096, 1408], P('req', 'tp'), may hold values from -24 to 24
- ln1_gain: float32 [1408], replicated, may hold values from 0.1 to 1.9
- ln1_bias: float32 [1408], replicated, may hold values from -3 to 3
- qkv_weight: bfloat16 [3, 1408, 1408], P(None, None, 'tp'), may hold values from -6 to 6
- out_weight: bfloat16 [1408, 1408], P('tp'), may hold values from -0.15625 to 0.15625
- ln2_gain: float32 [1408], replicated, may hold values from 0.25 to 1.75
- ln2_bias: float32 [1408], replicated, may hold values from -3 to 3
- merger_weight: bfloat16 [5632, 3584], P('req', 'tp'), may hold values from -0.078125 to 0.078125
- group_segments: int32 [8, 128], P('req'), may hold values from 0 to 7, never falling along the last dimension, each value on 1 to 41 neighbouring positions
- owners: int32 [1024, 1], P('req'), may hold values from 0 to 7; in each aligned block of 128 rows (0 to 127, 128 to 255, ...) at most 32 rows name the same one
Outputs:
- received: bfloat16 [2048, 3584], P('req', 'tp')
Inputs may be any that keep to these rules, and one draw needn't show every extreme that they name: `group_segments`: never falling along a request's groups; every picture has 1 to 41 groups and one has exactly 41. `owners`: among the 128 groups of one request no owner appears more than 32 times; in every draw some request sends exactly 32 to some owner.
All inputs are finite; a program needn't handle non-finite values.
Results may differ from a plain program's by a relative error of at most 0.009.
Values may be sent and summed in bfloat16 or wider, within the bound.
A program may use at most 128 MiB of HBM per device.

v0:
```python
import jax
import jax.numpy as jnp
from jax import lax
from jax.sharding import PartitionSpec as P

HEAD_DIM = 88


epsilon = 1e-06


def local(
    tokens,
    ln1_gain,
    ln1_bias,
    qkv_weight,
    out_weight,
    ln2_gain,
    ln2_bias,
    merger_weight,
    group_segments,
    owners,
):
    tp_count = lax.axis_size("tp")
    req_count = lax.axis_size("req")
    col_width = tokens.shape[1]
    full_width = col_width * tp_count
    tok_count = tokens.shape[0]
    group_count = tok_count // 4
    out_cols = merger_weight.shape[1]
    gathered = lax.all_gather(tokens, "tp", axis=1, tiled=True).astype(jnp.float32)
    input_mean = jnp.mean(gathered, axis=1, keepdims=True)
    centered = gathered - input_mean
    input_var = jnp.mean(centered * centered, axis=1, keepdims=True)
    normed = (centered * lax.rsqrt(input_var + epsilon) * ln1_gain + ln1_bias).astype(jnp.bfloat16)
    combined = jnp.einsum("td,cdh->cth", normed, qkv_weight, preferred_element_type=jnp.float32)
    combined = combined.astype(jnp.bfloat16).reshape(3, tok_count, -1, HEAD_DIM)
    queries, key_heads, value_heads = (combined[0], combined[1], combined[2])
    segment_ids = jnp.repeat(group_segments[0], 4)
    same_picture = segment_ids[:, None] == segment_ids[None, :]
    scores = jnp.einsum(
        "qhd,khd->hqk", queries, key_heads, preferred_element_type=jnp.float32
    ) * HEAD_DIM ** (-0.5)
    scores = jnp.where(same_picture[None], scores, -1e30)
    row_max = jnp.max(scores, axis=2, keepdims=True)
    exponent = jnp.exp(scores - row_max)
    weights = (exponent / jnp.sum(exponent, axis=2, keepdims=True)).astype(jnp.bfloat16)
    context = jnp.einsum("hqk,khd->qhd", weights, value_heads, preferred_element_type=jnp.float32)
    context = context.astype(jnp.bfloat16).reshape(tok_count, -1)
    partial_value = jnp.dot(context, out_weight, preferred_element_type=jnp.float32)
    attended = lax.psum_scatter(
        partial_value.astype(jnp.bfloat16), "tp", scatter_dimension=1, tiled=True
    ).astype(jnp.float32)
    hidden = tokens.astype(jnp.float32) + attended
    row_total = lax.psum(jnp.sum(hidden, axis=1), "tp")
    row_mean = (row_total / full_width)[:, None]
    shifted = hidden - row_mean
    row_spread = lax.psum(jnp.sum(shifted * shifted, axis=1), "tp")
    variance = (row_spread / full_width)[:, None]
    offset = lax.axis_index("tp") * col_width
    gain_part = lax.dynamic_slice_in_dim(ln2_gain, offset, col_width)
    bias_part = lax.dynamic_slice_in_dim(ln2_bias, offset, col_width)
    patches = (shifted * lax.rsqrt(variance + epsilon) * gain_part + bias_part).astype(jnp.bfloat16)
    grouped = patches.reshape(group_count, 4, col_width)
    full_groups = lax.all_gather(grouped, "tp", axis=2, tiled=True)
    merged = full_groups.reshape(group_count, 4 * full_width)
    projected = jnp.dot(
        merged,
        lax.all_gather(merger_weight, "req", axis=0, tiled=True),
        preferred_element_type=jnp.float32,
    )
    projected = projected.astype(jnp.bfloat16)
    capacity = max(2, 2 * group_count // req_count)
    slot_count = req_count * capacity
    target = owners[:, 0]
    owner_ids = jnp.arange(req_count, dtype=jnp.int32)
    owner_hits = (target[:, None] == owner_ids[None, :]).astype(jnp.int32)
    before = jnp.cumsum(owner_hits, axis=0) - owner_hits
    slot_rank = jnp.sum(before * owner_hits, axis=1)
    slot_index = target * capacity + slot_rank
    placing = (slot_index[None, :] == jnp.arange(slot_count, dtype=jnp.int32)[:, None]).astype(
        jnp.bfloat16
    )
    outgoing = jnp.dot(placing, projected, preferred_element_type=jnp.float32).astype(jnp.bfloat16)
    outgoing = outgoing.reshape(req_count, capacity, out_cols)
    arrived = lax.all_to_all(outgoing, "req", split_axis=0, concat_axis=0, tiled=True)
    return arrived.reshape(slot_count, out_cols)


def solution(mesh):
    in_specs = (
        P("req", "tp"),
        P(),
        P(),
        P(None, None, "tp"),
        P("tp", None),
        P(),
        P(),
        P("req", "tp"),
        P("req", None),
        P("req", None),
    )
    out_specs = P("req", "tp")
    return jax.shard_map(local, mesh=mesh, in_specs=in_specs, out_specs=out_specs, check_vma=False)
```

profile of v0, /device:TPU:0, one launch (start us, length us, event | category | flops | bytes accessed | tf_op | source)
XLA Modules:
  0.0 292.3 jit_solution(9198143594576457192)
XLA Ops:
  7.3 0.9 broadcast_in_dim.14
  8.3 0.9 broadcast_compare_fusion
  9.3 21.3 %all-gather.4.cloned.1.call-done = bf16[512,1408]{0,1:T(8,128)(2,1)} async-done(((bf16[512,352]{0,1:T(8,128)(2,1)}), bf16[512,1408]{0,1:T(8,128)(2,1)}) %all-gather.4.cloned.1.call-update) | async-done | bytes 1441808 | tf_op jit(solution)/shard_map/all_gather | solution.py:31
  30.6 1.7 convert_reduce_fusion
  32.3 1.8 fusion.4
  34.2 2.0 fusion.18
  36.2 0.9 fusion.30
  37.1 4.8 %fusion.31 = (f32[4,512]{1,0:T(4,128)S(1)}, f32[4,512,512]{1,2,0:T(8,128)}) fusion(pred[512,512]{0,1:T(8,128)(4,1)} %broadcast_compare_fusion, bf16[512,4,88]{0,2,1:T(8,128)(2,1)} %bitcast.34, bf16[512,4,88]{0,2,1:T(8,128)(2,1)} %bitcast.33), kind=kOutput, calls=%fused_computation.48 | convolution fusion | flops 188744192 | bytes 5185536 | tf_op jit(solution)/shard_map/sub | solution.py:46
  41.9 2.8 fusion.21
  44.7 2.1 convolution_convert_fusion
  48.4 25.9 %reduce-scatter.2.cloned.1.call-done = bf16[512,352]{0,1:T(8,128)(2,1)} async-done(((bf16[512,1408]{0,1:T(8,128)(2,1)}), bf16[512,352]{0,1:T(8,128)(2,1)}) %reduce-scatter.2.cloned.1.call-update) | async-done | bytes 360464 | tf_op jit(solution)/shard_map/reduce_scatter | solution.py:51
  74.3 1.1 fusion.23
  75.4 5.8 %psum.14 = f32[512]{0:T(512)S(1)} all-reduce(f32[512]{0:T(512)S(1)} %fusion.23), channel_id=1, replica_groups=mesh['req'=8,'tp'=4] {'tp'}, use_global_device_ids=true, to_apply=%region_8.9 | all-reduce | flops 512 | bytes 4096 | tf_op jit(solution)/shard_map/psum | solution.py:55
  81.2 1.1 multiply_reduce_fusion
  82.3 5.7 %psum.15 = f32[512]{0:T(512)S(1)} all-reduce(f32[512]{0:T(512)S(1)} %multiply_reduce_fusion), channel_id=1, replica_groups=mesh['req'=8,'tp'=4] {'tp'}, use_global_device_ids=true, to_apply=%region_10.11 | all-reduce | flops 512 | bytes 4096 | tf_op jit(solution)/shard_map/psum | solution.py:58
  88.0 1.9 add_convert_fusion
  89.9 1.2 copy.19
  91.1 0.9 reshape.86
  92.0 2.1 copy.20
  95.1 19.4 %all-gather.6.cloned.1.call-done = bf16[128,4,1408]{0,1,2:T(4,128)(2,1)} async-done(((bf16[128,4,352]{0,1,2:T(4,128)(2,1)}), bf16[128,4,1408]{0,1,2:T(4,128)(2,1)}) %all-gather.6.cloned.1.call-update) | async-done | bytes 1441808 | tf_op jit(solution)/shard_map/all_gather | solution.py:65
  114.5 2.7 copy.21
  117.2 145.7 %all-gather.8.cloned.1.call-done = bf16[5632,896]{1,0:T(8,128)(2,1)} async-done(((bf16[704,896]{1,0:T(8,128)(2,1)}), bf16[5632,896]{1,0:T(8,128)(2,1)}) %all-gather.8.cloned.1.call-update) | async-done | bytes 10092560 | tf_op jit(solution)/shard_map/all_gather | solution.py:69
  262.8 6.3 %convolution_convert_fusion.2 = bf16[256,896]{1,0:T(8,128)(2,1)S(1)} fusion(bf16[128,5632]{0,1:T(8,128)(2,1)} %bitcast.29, bf16[5632,896]{1,0:T(8,128)(2,1)} %all-gather.8.cloned.1.call-done, s32[128]{0:T(128)S(1)} %multiply_add_fusion), kind=kOutput, calls=%fused_computation.25 | convolution fusion | flops 1350942720 | bytes 11993600 | tf_op jit(solution)/shard_map/dot_general | solution.py:84
  269.1 15.9 %all_to_all.5 = bf16[8,32,896]{2,1,0:T(8,128)(2,1)S(1)} all-to-all(bf16[8,32,896]{2,1,0:T(8,128)(2,1)S(1)} %bitcast.31), channel_id=1, replica_groups=mesh['req'=8,'tp'=4] {'req'}, dimensions={0} | all-to-all | bytes 917504 | tf_op jit(solution)/shard_map/all_to_all | solution.py:86
  (34 shorter events, 4.3 us)
Async XLA Ops:
  6.5 27.6 %copy-start = (bf16[3,1408,352]{1,2,0:T(8,128)(2,1)S(1)}, bf16[3,1408,352]{1,2,0:T(8,128)(2,1)}, u32[]{:S(2)}) copy-start(bf16[3,1408,352]{1,2,0:T(8,128)(2,1)} %param.13) | copy-start | bytes 8921092
  6.5 27.6 %copy-start.6 = (f32[1408]{0:T(1024)S(1)}, f32[1408]{0:T(1024)}, u32[]{:S(2)}) copy-start(f32[1408]{0:T(1024)} %param.11) | copy-start | bytes 16900
  6.5 27.6 %copy-start.5 = (f32[1408]{0:T(1024)S(1)}, f32[1408]{0:T(1024)}, u32[]{:S(2)}) copy-start(f32[1408]{0:T(1024)} %param.12) | copy-start | bytes 16900
  6.5 24.0 %all-gather.4.cloned.1.call-start = ((), (), s32[]{:S(2)}) async-start(), calls=%async_computation.2 | async-start | bytes 1802240 | tf_op jit(solution)/shard_map/all_gather | solution.py:31
  7.3 67.0 %reduce-scatter.2.cloned.1.call-start = ((), (), s32[]{:S(2)}) async-start(), calls=%async_computation.3 | async-start | bytes 1802240 | tf_op jit(solution)/shard_map/reduce_scatter | solution.py:51
  30.6 3.6 %copy-start.1 = (bf16[512,1408]{0,1:T(8,128)(2,1)S(1)}, bf16[512,1408]{0,1:T(8,128)(2,1)}, u32[]{:S(2)}) copy-start(bf16[512,1408]{0,1:T(8,128)(2,1)} %all-gather.4.cloned.1.call-done) | copy-start | bytes 4325380
  41.9 2.8 copy-start.3
  44.7 29.6 %copy-start.2 = (bf16[512,352]{0,1:T(8,128)(2,1)S(1)}, bf16[512,352]{0,1:T(8,128)(2,1)}, u32[]{:S(2)}) copy-start(bf16[512,352]{0,1:T(8,128)(2,1)} %param.10) | copy-start | bytes 1081348
  46.8 67.7 %all-gather.6.cloned.1.call-start = ((), (), s32[]{:S(2)}) async-start(), calls=%async_computation.4 | async-start | bytes 1802240 | tf_op jit(solution)/shard_map/all_gather | solution.py:65
  75.4 19.3 %copy-start.4 = (s32[128,1]{0,1:T(1,128)S(1)}, s32[128,1]{0,1:T(1,128)}, u32[]{:S(2)}) copy-start(s32[128,1]{0,1:T(1,128)} %param.19) | copy-start | bytes 1540
  94.1 168.8 %all-gather.8.cloned.1.call-start = ((), (), s32[]{:S(2)}) async-start(), calls=%async_computation.5 | async-start | bytes 11354112 | tf_op jit(solution)/shard_map/all_gather | solution.py:69
Sparse Core Ops, SparseCore 0:
  8.9 21.6 all-gather.3
  46.9 27.3 reduce-scatter.1
  94.2 20.2 all-gather.5
  116.8 146.0 all-gather.7
where the time goes:
time: 293 us; the launch traced here: 292 us
  waiting for transfers between devices  214 us (73%)
  blocking collectives  27.3 us (9%)
  matrix products  17.9 us (6%)
  between operations  13.2 us (5%)
  local copies, waits for them, and re-layouts  11.1 us (4%)
  other arithmetic  9.11 us (3%)
    all_gather x1, waiting for transfers between devices, local(): lax.all_gather(merger_weight, 'req', axis=0, tiled=True)  146 us
    reduce_scatter x1, waiting for transfers between devices, local(): lax.psum_scatter(partial_value.astype(jnp.bfloat16), 'tp', scatter_dimens...  25.9 us
    all_gather x1, waiting for transfers between devices, local(): lax.all_gather(tokens, 'tp', axis=1, tiled=True).astype(jnp.float32)  21.3 us
    all_gather x1, waiting for transfers between devices, local(): full_groups = lax.all_gather(grouped, 'tp', axis=2, tiled=True)  19.4 us
    all_to_all x1, blocking collectives, local(): lax.all_to_all(outgoing, 'req', split_axis=0, concat_axis=0, tiled=True)  15.9 us
    dot_general x1, matrix products, local(): jnp.dot(placing, projected, preferred_element_type=jnp.float32)  6.26 us
  transfers between devices with their start and end apart: 4, of which 4 were waited for; matrix products, arithmetic and copies ran while one was open for 2% of the time, Pallas kernels for 0%

commit v1 on v0

v1 whole, which is shorter than its diff:
```python
import jax
import jax.numpy as jnp
from jax import lax
from jax.sharding import PartitionSpec as P

HEAD_DIM = 88


epsilon = 1e-06


def layer_norm(values, gain, bias):
    mean = jnp.mean(values, axis=1, keepdims=True)
    centered = values - mean
    variance = jnp.mean(centered * centered, axis=1, keepdims=True)
    return (centered * lax.rsqrt(variance + epsilon) * gain + bias).astype(jnp.bfloat16)


def local(
    tokens,
    ln1_gain,
    ln1_bias,
    qkv_weight,
    out_weight,
    ln2_gain,
    ln2_bias,
    merger_weight,
    group_segments,
    owners,
):
    tp_count = lax.axis_size("tp")
    req_count = lax.axis_size("req")
    tp_index = lax.axis_index("tp")
    req_index = lax.axis_index("req")
    half = req_count // 2
    upper = req_index // half
    tok_count = tokens.shape[0]
    width = tokens.shape[1] * tp_count
    row_count = tok_count // tp_count
    group_count = tok_count // 4
    own_groups = group_count // tp_count
    out_cols = merger_weight.shape[1]
    gathered = lax.all_gather(tokens, "tp", axis=1, tiled=True)
    gathered, merger_part = lax.optimization_barrier((gathered, merger_weight))
    halves = [list(range(half)), list(range(half, req_count))]
    kept_weight = lax.all_gather(
        merger_part, "req", axis=0, tiled=True, axis_index_groups=halves
    )
    normed = layer_norm(gathered.astype(jnp.float32), ln1_gain, ln1_bias)
    combined = jnp.einsum("td,cdh->cth", normed, qkv_weight, preferred_element_type=jnp.float32)
    combined = combined.astype(jnp.bfloat16).reshape(3, tok_count, -1, HEAD_DIM)
    queries, key_heads, value_heads = (combined[0], combined[1], combined[2])
    segment_ids = jnp.repeat(group_segments[0], 4)
    same_picture = segment_ids[:, None] == segment_ids[None, :]
    scores = jnp.einsum(
        "qhd,khd->hqk", queries, key_heads, preferred_element_type=jnp.float32
    ) * HEAD_DIM ** (-0.5)
    scores = jnp.where(same_picture[None], scores, -1e30)
    row_max = jnp.max(scores, axis=2, keepdims=True)
    exponent = jnp.exp(scores - row_max)
    weights = (exponent / jnp.sum(exponent, axis=2, keepdims=True)).astype(jnp.bfloat16)
    context = jnp.einsum("hqk,khd->qhd", weights, value_heads, preferred_element_type=jnp.float32)
    context = context.astype(jnp.bfloat16).reshape(tok_count, -1)
    partial_value = jnp.dot(context, out_weight, preferred_element_type=jnp.float32)
    pieces = partial_value.astype(jnp.bfloat16).reshape(tp_count, row_count, width)

    def rows_of(array, index):
        return lax.dynamic_index_in_dim(array, index, 0, keepdims=False)

    hidden = rows_of(gathered.reshape(tp_count, row_count, width), tp_index).astype(jnp.float32)
    hidden += rows_of(partial_value.reshape(tp_count, row_count, width), tp_index)
    for step in range(1, tp_count):
        leaving = rows_of(pieces, (tp_index + step) % tp_count)
        hidden += lax.ppermute(
            leaving, "tp", [(i, (i + step) % tp_count) for i in range(tp_count)]
        ).astype(jnp.float32)
    patches = layer_norm(hidden, ln2_gain, ln2_bias)
    merged = patches.reshape(own_groups, 2, 2 * width)
    swap = [(i, (i + half) % req_count) for i in range(req_count)]
    staying = lax.dynamic_index_in_dim(merged, upper, 1, keepdims=False)
    going = lax.dynamic_index_in_dim(merged, 1 - upper, 1, keepdims=False)
    coming = lax.ppermute(going, "req", swap)
    both = jnp.stack([staying, coming])
    full = lax.all_gather(both, "tp", axis=1, tiled=True)
    projected = jnp.dot(
        full.reshape(2 * group_count, 2 * width),
        kept_weight,
        preferred_element_type=jnp.float32,
    )
    arriving = lax.ppermute(projected[group_count:].astype(jnp.bfloat16), "req", swap)
    projected = projected[:group_count] + arriving.astype(jnp.float32)
    projected = projected.astype(jnp.bfloat16)
    capacity = max(2, 2 * group_count // req_count)
    slot_count = req_count * capacity
    target = owners[:, 0]
    same_owner = target[:, None] == target[None, :]
    place = jnp.arange(group_count, dtype=jnp.int32)
    earlier = same_owner & (place[None, :] < place[:, None])
    slot_rank = jnp.sum(earlier.astype(jnp.int32), axis=1)
    slot_index = target * capacity + slot_rank
    placing = (slot_index[None, :] == jnp.arange(slot_count, dtype=jnp.int32)[:, None]).astype(
        jnp.bfloat16
    )
    outgoing = jnp.dot(placing, projected, preferred_element_type=jnp.float32).astype(jnp.bfloat16)
    outgoing = outgoing.reshape(req_count, capacity, out_cols)
    arrived = lax.all_to_all(outgoing, "req", split_axis=0, concat_axis=0, tiled=True)
    return arrived.reshape(slot_count, out_cols)


def solution(mesh):
    in_specs = (
        P("req", "tp"),
        P(),
        P(),
        P(None, None, "tp"),
        P("tp", None),
        P(),
        P(),
        P("req", "tp"),
        P("req", None),
        P("req", None),
    )
    out_specs = P("req", "tp")
    return jax.shard_map(local, mesh=mesh, in_specs=in_specs, out_specs=out_specs, check_vma=False)
```

time: 293 us -> 240 us (0.82)
  waiting for transfers between devices: 214 us -> 169 us
  blocking collectives: 27.3 us -> 16.5 us
  starting transfers between devices: 0.12 us -> 7.06 us
    all_gather x3, waiting for transfers between devices: 186 us -> 136 us  [the longest x1 94.5 us: local(): lax.all_gather(merger_part, 'req', axis=0, tiled=True, axis_index_groups=...]
    ppermute x0 -> x5, waiting for transfers between devices: none -> 31.2 us  [the longest x3 12.1 us: local(): lax.ppermute(leaving, 'tp', [(i, (i + step) % tp_count) for i in range(tp...]
    reduce_scatter x1 -> x0, waiting for transfers between devices: 25.9 us -> none  [local(): lax.psum_scatter(partial_value.astype(jnp.bfloat16), 'tp', scatter_dimens...]
    psum x2 -> x0, blocking collectives: 11.4 us -> none  [the longest x1 5.76 us: local(): row_total = lax.psum(jnp.sum(hidden, axis=1), 'tp')]
    ppermute x0 -> x5, starting transfers between devices: none -> 6.97 us  [the longest x1 2.71 us: local(): coming = lax.ppermute(going, 'req', swap)]
    dot_general x1, matrix products: 6.26 us -> 0.29 us  [local(): jnp.dot(placing, projected, preferred_element_type=jnp.float32)]
    dot_general x0 -> x1, matrix products: none -> 4.54 us  [local(): jnp.dot(full.reshape(2 * group_count, 2 * width), kept_weight, preferred_...]
  transfers between devices with their start and end apart: 4 -> 8, of which waited for: 4 -> 8; matrix products, arithmetic and copies ran while one was open for 2% -> 2% of each run, Pallas kernels for 0% -> 0%
where the time goes in v1:
time: 240 us; the launch traced here: 239 us
  waiting for transfers between devices  169 us (70%)
  matrix products  17 us (7%)
  blocking collectives  16.5 us (7%)
  between operations  13.3 us (6%)
  other arithmetic  8.38 us (3%)
  local copies, waits for them, and re-layouts  8.24 us (3%)
  starting transfers between devices  7.06 us (3%)
    all_gather x1, waiting for transfers between devices, local(): lax.all_gather(merger_part, 'req', axis=0, tiled=True, axis_index_groups=...  94.5 us
    all_gather x1, waiting for transfers between devices, local(): gathered = lax.all_gather(tokens, 'tp', axis=1, tiled=True)  21.4 us
    all_gather x1, waiting for transfers between devices, local(): full = lax.all_gather(both, 'tp', axis=1, tiled=True)  20.6 us
    all_to_all x1, blocking collectives, local(): lax.all_to_all(outgoing, 'req', split_axis=0, concat_axis=0, tiled=True)  16.5 us
    ppermute x3, waiting for transfers between devices, local(): lax.ppermute(leaving, 'tp', [(i, (i + step) % tp_count) for i in range(tp...  12.1 us
    ppermute x1, waiting for transfers between devices, local(): lax.ppermute(projected[group_count:].astype(jnp.bfloat16), 'req', swap)  10.7 us
    ppermute x1, waiting for transfers between devices, local(): coming = lax.ppermute(going, 'req', swap)  8.38 us
    sub x1, matrix products, local(): exponent = jnp.exp(scores - row_max)  4.89 us
  transfers between devices with their start and end apart: 8, of which 8 were waited for; matrix products, arithmetic and copies ran while one was open for 2% of the time, Pallas kernels for 0%

profile of v1, /device:TPU:0, one launch (start us, length us, event | category | flops | bytes accessed | tf_op | source)
XLA Modules:
  0.0 239.5 jit_solution(7376993618558802189)
XLA Ops:
  9.2 21.4 %all-gather.4.cloned.1.call-done = bf16[512,1408]{0,1:T(8,128)(2,1)} async-done(((bf16[512,352]{0,1:T(8,128)(2,1)}), bf16[512,1408]{0,1:T(8,128)(2,1)}) %all-gather.4.cloned.1.call-update) | async-done | bytes 1441808 | tf_op jit(solution)/shard_map/all_gather | solution.py:43
  30.6 1.7 convert_reduce_fusion
  32.3 1.8 fusion.4
  34.2 2.0 fusion.18
  36.2 0.9 fusion.34
  37.1 4.9 %fusion.35 = (f32[4,512]{1,0:T(4,128)S(1)}, f32[4,512,512]{1,2,0:T(8,128)}) fusion(pred[512,512]{0,1:T(8,128)(4,1)} %broadcast_compare_fusion, bf16[512,4,88]{0,2,1:T(8,128)(2,1)} %bitcast.60, bf16[512,4,88]{0,2,1:T(8,128)(2,1)} %bitcast.59), kind=kOutput, calls=%fused_computation.58 | convolution fusion | flops 188744192 | bytes 5185536 | tf_op jit(solution)/shard_map/sub | solution.py:60
  42.0 2.8 %fusion.21 = bf16[4,88,512]{2,1,0:T(8,128)(2,1)S(1)} fusion(bf16[512,4,88]{0,2,1:T(8,128)(2,1)S(1)} %bitcast.58, f32[4,512,512]{1,2,0:T(8,128)} %get-tuple-element.20, f32[4,512]{1,0:T(4,128)S(1)} %get-tuple-element.19), kind=kOutput, calls=%fused_computation.25 | convolution fusion | flops 186826752 | bytes 4923392 | tf_op jit(solution)/shard_map/hqk,khd->qhd/dot_general | solution.py:62
  44.8 2.6 %fusion.36 = (bf16[512,1408]{1,0:T(8,128)(2,1)S(1)}, f32[512,1408]{1,0:T(8,128)}) fusion(bf16[512,352]{0,1:T(8,128)(2,1)S(1)} %bitcast.61, bf16[352,1408]{1,0:T(8,128)(2,1)S(1)} %copy-done.2), kind=kOutput, calls=%fused_computation.59 | convolution fusion | flops 508231680 | bytes 5677056 | tf_op jit(solution)/shard_map/dot_general | solution.py:64
  47.3 0.9 dynamic-slice_bitcast_fusion.2
  48.8 1.2 collective-permute-start.2
  50.1 2.6 %copy.25 = bf16[512,1408]{1,0:T(8,128)(2,1)} copy(bf16[512,1408]{0,1:T(8,128)(2,1)} %all-gather.4.cloned.1.call-done) | data formatting | bytes 2883584 | tf_op jit(solution)/shard_map/reshape | solution.py:70
  52.6 5.9 %collective-permute-done = bf16[128,1408]{1,0:T(8,128)(2,1)} collective-permute-done((bf16[128,1408]{1,0:T(8,128)(2,1)}, bf16[128,1408]{1,0:T(8,128)(2,1)}, u32[]{:S(2)}, u32[]{:S(2)}) %collective-permute-start) | collective-permute-done | bytes 360480 | tf_op jit(solution)/shard_map/ppermute | solution.py:74
  58.5 1.6 collective-permute-done.1
  60.1 4.7 %collective-permute-done.2 = bf16[128,1408]{1,0:T(8,128)(2,1)} collective-permute-done((bf16[128,1408]{1,0:T(8,128)(2,1)S(1)}, bf16[128,1408]{1,0:T(8,128)(2,1)}, u32[]{:S(2)}, u32[]{:S(2)}) %collective-permute-start.2) | collective-permute-done | bytes 360480 | tf_op jit(solution)/shard_map/ppermute | solution.py:74
  64.7 1.8 fusion.32
  67.8 1.2 reshape.110
  69.8 2.7 %collective-permute-start.3 = (bf16[32,2816]{1,0:T(8,128)(2,1)S(1)}, bf16[32,2816]{1,0:T(8,128)(2,1)S(1)}, u32[]{:S(2)}, u32[]{:S(2)}) collective-permute-start(bf16[32,2816]{1,0:T(8,128)(2,1)S(1)} %bitcast.62), channel_id=1, source_target_pairs={{0,16},{4,20},{8,24},{12,28},{16,0},{20,4},{24,8},{28,12},{1,17},{... | collective-permute-start | bytes 540680 | tf_op jit(solution)/shard_map/ppermute | solution.py:82
  72.5 8.4 %collective-permute-done.3 = bf16[32,2816]{1,0:T(8,128)(2,1)S(1)} collective-permute-done((bf16[32,2816]{1,0:T(8,128)(2,1)S(1)}, bf16[32,2816]{1,0:T(8,128)(2,1)S(1)}, u32[]{:S(2)}, u32[]{:S(2)}) %collective-permute-start.3) | collective-permute-done | bytes 180256 | tf_op jit(solution)/shard_map/ppermute | solution.py:82
  82.4 20.6 %all-gather.6.cloned.1.call-done = bf16[2,128,2816]{2,1,0:T(8,128)(2,1)} async-done(((bf16[2,32,2816]{2,1,0:T(8,128)(2,1)}), bf16[2,128,2816]{2,1,0:T(8,128)(2,1)}) %all-gather.6.cloned.1.call-update) | async-done | bytes 1441808 | tf_op jit(solution)/shard_map/all_gather | solution.py:84
  103.0 94.5 %all-gather.8.cloned.1.call-done = bf16[2816,896]{1,0:T(8,128)(2,1)} async-done(((bf16[704,896]{1,0:T(8,128)(2,1)}), bf16[2816,896]{1,0:T(8,128)(2,1)}) %all-gather.8.cloned.1.call-update) | async-done | bytes 5046288 | tf_op jit(solution)/shard_map/all_gather | solution.py:46
  197.4 4.5 %fusion.37 = f32[256,896]{1,0:T(8,128)S(1)} fusion(bf16[256,2816]{1,0:T(8,128)(2,1)} %bitcast.65, bf16[2816,896]{1,0:T(8,128)(2,1)} %all-gather.8.cloned.1.call-done), kind=kOutput, calls=%fused_computation.60 | convolution fusion | flops 1291845632 | bytes 7405568 | tf_op jit(solution)/shard_map/dot_general | solution.py:85
  202.0 2.5 %collective-permute-start.4 = (bf16[128,896]{1,0:T(8,128)(2,1)S(1)}, bf16[128,896]{1,0:T(8,128)(2,1)S(1)}, u32[]{:S(2)}, u32[]{:S(2)}) collective-permute-start(bf16[128,896]{1,0:T(8,128)(2,1)S(1)} %slice.34), channel_id=1, source_target_pairs={{0,16},{4,20},{8,24},{12,28},{16,0},{20,4},{24,8},{28,12},{1,17},{... | collective-permute-start | bytes 688136 | tf_op jit(solution)/shard_map/ppermute | solution.py:90
  204.7 10.7 %collective-permute-done.4 = bf16[128,896]{1,0:T(8,128)(2,1)S(1)} collective-permute-done((bf16[128,896]{1,0:T(8,128)(2,1)S(1)}, bf16[128,896]{1,0:T(8,128)(2,1)S(1)}, u32[]{:S(2)}, u32[]{:S(2)}) %collective-permute-start.4) | collective-permute-done | bytes 229408 | tf_op jit(solution)/shard_map/ppermute | solution.py:90
  215.7 16.5 %all_to_all.5 = bf16[8,32,896]{2,1,0:T(8,128)(2,1)S(1)} all-to-all(bf16[8,32,896]{2,1,0:T(8,128)(2,1)S(1)} %bitcast.56), channel_id=1, replica_groups=mesh['req'=8,'tp'=4] {'req'}, dimensions={0} | all-to-all | bytes 917504 | tf_op jit(solution)/shard_map/all_to_all | solution.py:106
  (42 shorter events, 7.9 us)
Async XLA Ops:
  6.5 27.6 %copy-start = (bf16[3,1408,352]{1,2,0:T(8,128)(2,1)S(1)}, bf16[3,1408,352]{1,2,0:T(8,128)(2,1)}, u32[]{:S(2)}) copy-start(bf16[3,1408,352]{1,2,0:T(8,128)(2,1)} %param.13) | copy-start | bytes 8921092
  6.5 27.6 %copy-start.6 = (f32[1408]{0:T(1024)S(1)}, f32[1408]{0:T(1024)}, u32[]{:S(2)}) copy-start(f32[1408]{0:T(1024)} %param.11) | copy-start | bytes 16900
  6.5 27.6 %copy-start.5 = (f32[1408]{0:T(1024)S(1)}, f32[1408]{0:T(1024)}, u32[]{:S(2)}) copy-start(f32[1408]{0:T(1024)} %param.12) | copy-start | bytes 16900
  6.5 24.0 %all-gather.4.cloned.1.call-start = ((), (), s32[]{:S(2)}) async-start(), calls=%async_computation.1 | async-start | bytes 1802240 | tf_op jit(solution)/shard_map/all_gather | solution.py:43
  7.3 95.7 %all-gather.6.cloned.1.call-start = ((), (), s32[]{:S(2)}) async-start(), calls=%async_computation.2 | async-start | bytes 1802240 | tf_op jit(solution)/shard_map/all_gather | solution.py:84
  30.6 3.6 %copy-start.1 = (bf16[512,1408]{0,1:T(8,128)(2,1)S(1)}, bf16[512,1408]{0,1:T(8,128)(2,1)}, u32[]{:S(2)}) copy-start(bf16[512,1408]{0,1:T(8,128)(2,1)} %all-gather.4.cloned.1.call-done) | copy-start | bytes 4325380
  42.0 2.8 %copy-start.2 = (bf16[352,1408]{1,0:T(8,128)(2,1)S(1)}, bf16[352,1408]{1,0:T(8,128)(2,1)}, u32[]{:S(2)}) copy-start(bf16[352,1408]{1,0:T(8,128)(2,1)} %param.14) | copy-start | bytes 2973700
  48.3 10.2 %collective-permute-start = (bf16[128,1408]{1,0:T(8,128)(2,1)}, bf16[128,1408]{1,0:T(8,128)(2,1)}, u32[]{:S(2)}, u32[]{:S(2)}) collective-permute-start(bf16[128,1408]{1,0:T(8,128)(2,1)} %get-tuple-element.11), channel_id=1, source_target_pairs={{0,1},{1,2},{2,3},{3,0},{4,5},{5,6},{6,7},{7,4},{8,9},{9,10},{10,1... | collective-permute-start | bytes 1081352 | tf_op jit(solution)/shard_map/ppermute | solution.py:74
  48.5 11.6 %collective-permute-start.1 = (bf16[128,1408]{1,0:T(8,128)(2,1)}, bf16[128,1408]{1,0:T(8,128)(2,1)}, u32[]{:S(2)}, u32[]{:S(2)}) collective-permute-start(bf16[128,1408]{1,0:T(8,128)(2,1)} %get-tuple-element.13), channel_id=1, source_target_pairs={{0,2},{1,3},{2,0},{3,1},{4,6},{5,7},{6,4},{7,5},{8,10},{9,11},{10,... | collective-permute-start | bytes 1081352 | tf_op jit(solution)/shard_map/ppermute | solution.py:74
  48.8 15.9 %collective-permute-start.2 = (bf16[128,1408]{1,0:T(8,128)(2,1)S(1)}, bf16[128,1408]{1,0:T(8,128)(2,1)}, u32[]{:S(2)}, u32[]{:S(2)}) collective-permute-start(bf16[128,1408]{1,0:T(8,128)(2,1)S(1)} %get-tuple-element.12), channel_id=1, source_target_pairs={{0,3},{1,0},{2,1},{3,2},{4,7},{5,4},{6,5},{7,6},{8,11},{9,8},{10,9... | collective-permute-start | bytes 1081352 | tf_op jit(solution)/shard_map/ppermute | solution.py:74
  50.1 16.8 %copy-start.3 = (f32[1408]{0:T(1024)S(1)}, f32[1408]{0:T(1024)}, u32[]{:S(2)}) copy-start(f32[1408]{0:T(1024)} %param.16) | copy-start | bytes 16900
  50.1 16.8 %copy-start.4 = (f32[1408]{0:T(1024)S(1)}, f32[1408]{0:T(1024)}, u32[]{:S(2)}) copy-start(f32[1408]{0:T(1024)} %param.15) | copy-start | bytes 16900
  69.8 11.1 %collective-permute-start.3 = (bf16[32,2816]{1,0:T(8,128)(2,1)S(1)}, bf16[32,2816]{1,0:T(8,128)(2,1)S(1)}, u32[]{:S(2)}, u32[]{:S(2)}) collective-permute-start(bf16[32,2816]{1,0:T(8,128)(2,1)S(1)} %bitcast.62), channel_id=1, source_target_pairs={{0,16},{4,20},{8,24},{12,28},{16,0},{20,4},{24,8},{28,12},{1,17},{... | collective-permute-start | bytes 540680 | tf_op jit(solution)/shard_map/ppermute | solution.py:82
  81.7 115.8 %all-gather.8.cloned.1.call-start = ((), (), s32[]{:S(2)}) async-start(), calls=%async_computation.3 | async-start | bytes 6307840 | tf_op jit(solution)/shard_map/all_gather | solution.py:46
  197.4 7.1 %copy-start.7 = (s32[128,1]{0,1:T(1,128)S(1)}, s32[128,1]{0,1:T(1,128)}, u32[]{:S(2)}) copy-start(s32[128,1]{0,1:T(1,128)} %param.19) | copy-start | bytes 1540
  202.0 13.4 %collective-permute-start.4 = (bf16[128,896]{1,0:T(8,128)(2,1)S(1)}, bf16[128,896]{1,0:T(8,128)(2,1)S(1)}, u32[]{:S(2)}, u32[]{:S(2)}) collective-permute-start(bf16[128,896]{1,0:T(8,128)(2,1)S(1)} %slice.34), channel_id=1, source_target_pairs={{0,16},{4,20},{8,24},{12,28},{16,0},{20,4},{24,8},{28,12},{1,17},{... | collective-permute-start | bytes 688136 | tf_op jit(solution)/shard_map/ppermute | solution.py:90
Sparse Core Ops, SparseCore 0:
  8.9 21.6 all-gather.3
  81.8 21.1 all-gather.5
  104.5 92.8 all-gather.7
